TPU v7x, 128 devices: a whole 4x4x4 slice. The times are simulated.
128 devices in a mesh: genome: 64 (over x, z, y_hi, core), sample: 2 (over y_lo).
Axes of the slice: x: 4, y: 4 (y_hi: 2, y_lo: 2; y = y_hi * 2 + y_lo), z: 4, core: 2. Of those that a mesh axis runs over, the one named last changes fastest.
Arguments:
- dosage: bfloat16 [512, 262144], P(('genome', 'sample'))
- missing: int32 [262144], replicated, may hold values from 0 to 128
- positions: int32 [262144], replicated, may hold values from 0 to 512, as said below
- chrom_end: int32 [262144], replicated, may hold values 0 or 1
- pair_pattern: int32 [1024, 5], replicated, may hold values 0 or 1
Outputs:
- ld: bfloat16 [262144, 1280], P(('genome', 'sample'))
Inputs may be any that keep to these rules, and one draw needn't show every extreme that they name: positions start at 0 and never fall; from one variant to the next they rise by 0 or 1.
All inputs are finite; a program needn't handle non-finite values.
Results may differ from a plain program's by a relative error of at most 0.0026.
Values may be sent and summed in bfloat16 or wider, within the bound.
No kernel may reach another device: no remote copies, remote signals or barrier semaphores. Data moves between devices by JAX's collectives and lax.ppermute only.
A program may use at most 192 MiB of HBM per device.

v0:
```python
import jax
import jax.numpy as jnp
from jax import lax
from jax.experimental import pallas as pl
from jax.experimental.pallas import tpu as pltpu
from jax.sharding import PartitionSpec as P

SAMPLES = 512
BLK = 256
BAND = 4
RIM = BAND * BLK
WIDTH = RIM + BLK
AXES = ("genome", "sample")
FAR = 1e9


def standardize(dosage_ref, count_ref, z_ref, block):
    cols = pl.ds(pl.multiple_of(block * BLK, BLK), BLK)
    values = dosage_ref[:, :, cols].astype(jnp.float32).reshape(SAMPLES, BLK)
    count = count_ref[block]
    mean = jnp.sum(values, axis=0, keepdims=True) / count
    centred = values - mean
    var = jnp.sum(centred * centred, axis=0, keepdims=True) / count
    z_ref[block] = (centred * (1.0 / jnp.sqrt(var + 1e-05))).astype(jnp.bfloat16)


def band_kernel(dosage_ref, count_ref, key_row_ref, scale_row_ref, key_col_ref, scale_col_ref, ld_ref, z_ref):
    i = pl.program_id(0)

    @pl.when(i == 0)
    def _():
        @pl.loop(0, BAND + 1)
        def _(block):
            standardize(dosage_ref, count_ref, z_ref, block)

    @pl.when(i < pl.num_programs(0) - 1)
    def _():
        standardize(dosage_ref, count_ref, z_ref, i + BAND + 1)

    left = z_ref[i].T
    key_a = key_col_ref[...]
    scale_a = scale_col_ref[...]
    for offset in range(BAND + 1):
        prod = jnp.dot(left, z_ref[i + offset], preferred_element_type=jnp.float32)
        for half in range(2):
            first = offset * BLK + half * 128
            key_j = key_row_ref[0, :, first : first + 128]
            scale_j = scale_row_ref[0, :, first : first + 128]
            keep = key_j <= key_a + 1.0
            if offset == 0:
                keep &= key_j >= key_a - 1.0
            ld = jnp.where(keep, prod[:, half * 128 : half * 128 + 128] * (scale_a * scale_j), 0.0)
            ld_ref[:, first : first + 128] = ld.astype(jnp.bfloat16)


def on_device(dosage, missing, positions, chrom_end, pair_pattern):
    nvar_all = dosage.shape[1]
    ndev = lax.axis_size("genome") * lax.axis_size("sample")
    nvar = nvar_all // ndev
    nblk = nvar // BLK
    slab = lax.axis_index(AXES)
    row_first = slab * nvar
    last = slab == ndev - 1

    blocks = dosage.reshape(-1, ndev, nvar).transpose(1, 0, 2)
    rim = jnp.concatenate([blocks[1:, :, :RIM], jnp.zeros_like(blocks[:1, :, :RIM])], axis=0)
    mine = lax.all_to_all(
        jnp.concatenate([blocks, rim], axis=2), AXES, split_axis=0, concat_axis=0, tiled=True
    )

    def extended(table, fill):
        own = lax.dynamic_slice_in_dim(table, row_first, nvar, 0)
        start = jnp.minimum(row_first + nvar, nvar_all - RIM)
        after = lax.dynamic_slice_in_dim(table, start, RIM, 0)
        return jnp.concatenate([own, jnp.where(last, fill, after)])

    count = (SAMPLES - extended(missing, 0)).astype(jnp.float32)
    ends = extended(chrom_end, 0)
    seg = jnp.cumsum(ends) - ends
    key = (extended(positions, 0) + 4 * seg).astype(jnp.float32)
    key = jnp.where(last & (jnp.arange(nvar + RIM) >= nvar), FAR, key)
    scale = 1.0 / jnp.sqrt(count)

    def window(table):
        grid = table.reshape(-1, BLK)
        return jnp.stack([grid[k : k + nblk] for k in range(BAND + 1)], axis=1)

    pattern = lax.dynamic_slice_in_dim(pair_pattern, slab * nblk, nblk, 0)
    key_row = jnp.where(pattern[:, :, None] == 1, window(key), FAR).reshape(nblk, 1, WIDTH)
    scale_row = window(scale).reshape(nblk, 1, WIDTH)
    key_col = jnp.broadcast_to(key[:nvar, None], (nvar, 128))
    scale_col = jnp.broadcast_to(scale[:nvar, None], (nvar, 128))

    whole = pl.BlockSpec(memory_space=pltpu.VMEM)
    row_spec = pl.BlockSpec((1, 1, WIDTH), lambda i: (i, 0, 0))
    col_spec = pl.BlockSpec((BLK, 128), lambda i: (i, 0))
    return pl.pallas_call(
        band_kernel,
        grid=(nblk,),
        in_specs=[whole, whole, row_spec, row_spec, col_spec, col_spec],
        out_specs=pl.BlockSpec((BLK, WIDTH), lambda i: (i, 0)),
        out_shape=jax.ShapeDtypeStruct((nvar, WIDTH), jnp.bfloat16),
        scratch_shapes=[pltpu.VMEM((nblk + BAND, SAMPLES, BLK), jnp.bfloat16)],
        compiler_params=pltpu.CompilerParams(vmem_limit_bytes=40 << 20),
    )(mine, count.reshape(-1, 1, BLK), key_row, scale_row, key_col, scale_col)


def solution(mesh):
    placed = (P(AXES, None), P(), P(), P(), P())
    return jax.shard_map(
        on_device,
        mesh=mesh,
        in_specs=placed,
        out_specs=P(AXES, None),
        check_vma=False,
    )
```

profile of v0, /device:TPU:1, one launch (start us, length us, event | category | flops | bytes accessed | tf_op | source)
XLA Modules:
  0.0 68.5 jit_solution(11362158494958947130)
XLA Ops:
  0.0 1.6 %slice.81 = bf16[127,4,1024]{2,1,0:T(4,128)(2,1)S(1)} slice(bf16[128,4,2048]{2,1,0:T(4,128)(2,1)} %bitcast.11), slice={[1:128], [0:4], [0:1024]} | slice | bytes 2080768 | tf_op jit(solution)/shard_map/slice | solution.py:66
  1.6 4.7 %fusion.1 = bf16[128,4,3072]{2,1,0:T(4,128)(2,1)} fusion(bf16[127,4,1024]{2,1,0:T(4,128)(2,1)S(1)} %slice.81, bf16[128,4,2048]{2,1,0:T(4,128)(2,1)} %bitcast.12), kind=kLoop, calls=%fused_computation.2 | loop fusion | flops 9437184 | bytes 6283264 | tf_op jit(solution)/shard_map/concatenate | solution.py:68
  6.3 11.5 %all-to-all-start = ((bf16[128,4,3072]{2,1,0:T(4,128)(2,1)}), bf16[128,4,3072]{2,1,0:T(4,128)(2,1)S(1)}, u32[]{:S(2)}, u32[]{:S(2)}) async-start(bf16[128,4,3072]{2,1,0:T(4,128)(2,1)} %fusion.1), calls=%async_computation | async-start | bytes 6291456 | tf_op jit(solution)/shard_map/all_to_all | solution.py:67
  17.8 0.7 %dynamic_slice.24 = s32[2048]{0:T(1024)S(1)} dynamic-slice(s32[262144]{0:T(1024)} %param.7, s32[]{:T(128)S(6)} %select_n.60), dynamic_slice_sizes={2048} | dynamic-slice | bytes 16388 | tf_op jit(solution)/shard_map/dynamic_slice | solution.py:72
  18.5 0.7 %dynamic_slice.26 = s32[2048]{0:T(1024)S(1)} dynamic-slice(s32[262144]{0:T(1024)} %param.8, s32[]{:T(128)S(6)} %select_n.60), dynamic_slice_sizes={2048} | dynamic-slice | bytes 16388 | tf_op jit(solution)/shard_map/dynamic_slice | solution.py:72
  19.2 0.8 %dynamic-slice_select_fusion = (s32[1024]{0:T(1024)S(1)}, s32[1024]{0:T(1024)S(1)}) fusion(s32[262144]{0:T(1024)} %param.8, s32[]{:T(128)S(6)} %select_n.62, pred[]{:T(512)S(6)} %eq.10, s32[262144]{0:T(1024)} %param.7), kind=kLoop, calls=%fused_computation.32 | loop fusion | flops 2048 | bytes 16389 | tf_op jit(solution)/shard_map/jit(_where)/select_n | solution.py:75
  20.0 0.3 reduce-window.9
  20.3 0.1 slice.82
  20.3 0.7 %dynamic_slice.21 = s32[2048]{0:T(1024)S(1)} dynamic-slice(s32[262144]{0:T(1024)} %param.6, s32[]{:T(128)S(6)} %select_n.60), dynamic_slice_sizes={2048} | dynamic-slice | bytes 16388 | tf_op jit(solution)/shard_map/dynamic_slice | solution.py:72
  21.0 0.8 %dynamic-slice_select_fusion.2 = s32[1024]{0:T(1024)S(1)} fusion(s32[262144]{0:T(1024)} %param.6, s32[]{:T(128)S(6)} %select_n.62, pred[]{:T(512)S(6)} %eq.10), kind=kLoop, calls=%fused_computation.35 | loop fusion | flops 1024 | bytes 8197 | tf_op jit(solution)/shard_map/jit(_where)/select_n | solution.py:75
  21.9 0.1 slice_reduce_fusion
  22.0 0.1 reshape.228
  22.1 0.1 broadcast.137
  22.3 0.1 stack.5
  22.4 0.8 %dynamic-slice_compare_fusion = pred[8,5]{0,1:T(8,128)(4,1)S(1)} fusion(s32[1024,5]{0,1:T(8,128)} %param.9, s32[]{:T(128)S(6)} %select_n.64), kind=kLoop, calls=%fused_computation.34 | loop fusion | flops 40 | bytes 204 | tf_op jit(solution)/shard_map/eq | solution.py:89
  23.2 0.1 broadcast_select_fusion
  23.4 0.1 add_bitcast_fusion
  23.5 36.0 %all-to-all-done.dosage_ref = bf16[128,4,3072]{2,1,0:T(4,128)(2,1)S(1)} async-done(((bf16[128,4,3072]{2,1,0:T(4,128)(2,1)}), bf16[128,4,3072]{2,1,0:T(4,128)(2,1)S(1)}, u32[]{:S(2)}, u32[]{:S(2)}) %all-to-all-start) | async-done | bytes 3145760 | tf_op jit(solution)/shard_map/all_to_all | solution.py:67
  59.4 0.3 broadcast_in_dim.43.key_col_ref
  59.8 0.3 broadcast_in_dim.44.scale_col_ref
  60.1 8.4 %shard_map.55 = bf16[2048,1280]{1,0:T(8,128)(2,1)} custom-call(bf16[128,4,3072]{2,1,0:T(4,128)(2,1)S(1)} %all-to-all-done.dosage_ref, f32[12,1,256]{2,1,0:T(1,128)S(1)} %bitcast.10, f32[8,1,1280]{2,1,0:T(1,128)S(1)} %copy.10.key_row_ref, f32[8,1,1280]{2,1,0:T(1,128)S(1)} %reshape.232.scale_row_ref, f32[2048,128]{1,0:T(8,128)S(1)} %broadcast_in_dim.43.key_col_ref, ...), custom_call_target="tpu_custom_call" | custom-call | tf_op jit(solution)/shard_map/pallas_call | solution.py:97
  (20 shorter events, 0.3 us)
Async XLA Ops:
  6.3 53.2 %all-to-all-start = ((bf16[128,4,3072]{2,1,0:T(4,128)(2,1)}), bf16[128,4,3072]{2,1,0:T(4,128)(2,1)S(1)}, u32[]{:S(2)}, u32[]{:S(2)}) async-start(bf16[128,4,3072]{2,1,0:T(4,128)(2,1)} %fusion.1), calls=%async_computation | async-start | bytes 6291456 | tf_op jit(solution)/shard_map/all_to_all | solution.py:67
where the time goes:
time: 69.1 us; the launch traced here: 68.5 us
  waiting for transfers between devices  36 us (52%)
  starting transfers between devices  11.5 us (17%)
  Pallas kernels  8.44 us (12%)
  other arithmetic  7.51 us (11%)
  local copies, waits for them, and re-layouts  4.96 us (7%)
    all_to_all x1, waiting for transfers between devices, on_device(): lax.all_to_all(jnp.concatenate([blocks, rim], axis=2), AXES, split_axis=0...  36 us
    all_to_all x1, starting transfers between devices, on_device(): lax.all_to_all(jnp.concatenate([blocks, rim], axis=2), AXES, split_axis=0...  11.5 us
    pallas_call x1, Pallas kernels, on_device(): pl.pallas_call(band_kernel, grid=(nblk,), in_specs=[whole, whole, row_spe...  8.44 us
    concatenate x1, other arithmetic, on_device(): jnp.concatenate([blocks, rim], axis=2)  4.67 us
    dynamic_slice x3, local copies, waits for them, and re-layouts, extended(): own = lax.dynamic_slice_in_dim(table, row_first, nvar, 0)  2.1 us
    slice x1, local copies, waits for them, and re-layouts, on_device(): blocks[1:, :, :RIM]  1.58 us
    select_n x2, other arithmetic, extended(): return jnp.concatenate([own, jnp.where(last, fill, after)])  1.56 us
  transfers between devices with their start and end apart: 1, of which 1 were waited for; matrix products, arithmetic and copies ran while one was open for 8% of the time, Pallas kernels for 0%

commit v1 on v0

v1 whole, which is shorter than its diff:
```python
import jax
import jax.numpy as jnp
from jax import lax
from jax.experimental import pallas as pl
from jax.experimental.pallas import tpu as pltpu
from jax.sharding import PartitionSpec as P

SAMPLES = 512
BLK = 256
BAND = 4
RIM = BAND * BLK
WIDTH = RIM + BLK
CHUNK = 64
PACKS = 4
AXES = ("genome", "sample")
FAR = 1e9


def pack_kernel(slabs_ref, sent_ref, held_ref, sem):
    ndev, _, nvar = slabs_ref.shape
    step = ndev // PACKS
    first, own, edge = pl.ds(0, RIM), pl.ds(0, nvar), pl.ds(nvar, RIM)
    reads = [
        pltpu.make_async_copy(slabs_ref.at[part], held_ref.at[part], sem.at[0, p])
        for p, part in enumerate(pl.ds(p * step, step) for p in range(PACKS))
    ]
    for read in reads:
        read.start()
    writes = []
    for p, read in enumerate(reads):
        read.wait()
        part = pl.ds(p * step, step)
        writes.append(pltpu.make_async_copy(held_ref.at[part], sent_ref.at[part, :, own], sem.at[1, p]))
        low = max(p * step, 1)
        count = (p + 1) * step - low
        writes.append(
            pltpu.make_async_copy(
                held_ref.at[pl.ds(low, count), :, first], sent_ref.at[pl.ds(low - 1, count), :, edge], sem.at[2, p]
            )
        )
        if p == 0:
            writes.append(
                pltpu.make_async_copy(
                    held_ref.at[pl.ds(0, 1), :, first], sent_ref.at[pl.ds(ndev - 1, 1), :, edge], sem.at[3, 0]
                )
            )
        for write in writes[2 * p + (p > 0) :]:
            write.start()
    for write in writes:
        write.wait()


def standardize(dosage_ref, count_ref, z_ref, block):
    cols = slice(block * BLK, (block + 1) * BLK)
    step = CHUNK * dosage_ref.shape[0] // SAMPLES
    chunks = [slice(g * CHUNK, (g + 1) * CHUNK) for g in range(SAMPLES // CHUNK)]

    def total(parts):
        part = sum(p.reshape(CHUNK // 8, 8, BLK).sum(axis=0) for p in parts)
        return part.sum(axis=0, keepdims=True)

    def dosages():
        for g, rows in enumerate(chunks):
            values = dosage_ref[g * step : (g + 1) * step, :, cols].astype(jnp.float32).reshape(CHUNK, BLK)
            z_ref[block, rows, :] = values.astype(jnp.bfloat16)
            yield values

    def centred(rows):
        return z_ref[block, rows, :].astype(jnp.float32) - mean

    count = count_ref[block]
    mean = total(dosages()) / count
    var = total(c * c for c in map(centred, chunks)) / count
    inverse = 1.0 / jnp.sqrt(var + 1e-05)
    for rows in chunks:
        z_ref[block, rows, :] = (centred(rows) * inverse).astype(jnp.bfloat16)


def column(row):
    return jnp.broadcast_to(row, (128, row.shape[1])).T


def band_rows(z_ref, key_row_ref, scale_row_ref, key_own_ref, scale_own_ref, ld_ref, block):
    rows = slice(block * BLK, (block + 1) * BLK)
    left = z_ref[block].T
    top = column(key_own_ref[block] + 1.0)
    scale_a = column(scale_own_ref[block])
    for offset in range(BAND + 1):
        prod = jnp.dot(left, z_ref[block + offset], preferred_element_type=jnp.float32)
        for half in range(BLK // 128):
            cols = slice(offset * BLK + half * 128, offset * BLK + half * 128 + 128)
            key_j = key_row_ref[block, :, cols]
            keep = key_j <= top
            if offset == 0:
                keep &= key_j >= top - 2.0
            weight = scale_a * scale_row_ref[block, :, cols]
            ld = jnp.where(keep, prod[:, half * 128 : half * 128 + 128] * weight, 0.0)
            ld_ref[rows, cols] = ld.astype(jnp.bfloat16)


def band_kernel(
    dosage_ref, count_ref, key_row_ref, scale_row_ref, key_own_ref, scale_own_ref, out_ref, z_ref, ld_ref, sem
):
    nblk = key_row_ref.shape[0]
    copies = []
    for block in range(BAND + 1):
        standardize(dosage_ref, count_ref, z_ref, block)
    for block in range(nblk):
        if block + 1 < nblk:
            standardize(dosage_ref, count_ref, z_ref, block + BAND + 1)
        band_rows(z_ref, key_row_ref, scale_row_ref, key_own_ref, scale_own_ref, ld_ref, block)
        rows = pl.ds(block * BLK, BLK)
        copies.append(pltpu.make_async_copy(ld_ref.at[rows], out_ref.at[rows], sem.at[block]))
        copies[-1].start()
    for copy in copies:
        copy.wait()


def on_device(dosage, missing, positions, chrom_end, pair_pattern):
    nvar_all = dosage.shape[1]
    ndev = lax.axis_size("genome") * lax.axis_size("sample")
    nvar = nvar_all // ndev
    nblk = nvar // BLK
    slab = lax.axis_index(AXES)
    row_first = slab * nvar
    last = slab == ndev - 1

    slabs = dosage.reshape(-1, ndev, nvar).transpose(1, 0, 2)
    anywhere = pl.BlockSpec(memory_space=pl.ANY)
    sent = pl.pallas_call(
        pack_kernel,
        in_specs=[anywhere],
        out_specs=anywhere,
        out_shape=jax.ShapeDtypeStruct((ndev, slabs.shape[1], nvar + RIM), dosage.dtype),
        scratch_shapes=[pltpu.VMEM(slabs.shape, dosage.dtype), pltpu.SemaphoreType.DMA((4, PACKS))],
        compiler_params=pltpu.CompilerParams(vmem_limit_bytes=56 << 20),
    )(slabs)
    mine = lax.all_to_all(sent, AXES, split_axis=0, concat_axis=0, tiled=True)

    def extended(table, fill):
        own = lax.dynamic_slice_in_dim(table, row_first, nvar, 0)
        start = jnp.minimum(row_first + nvar, nvar_all - RIM)
        after = lax.dynamic_slice_in_dim(table, start, RIM, 0)
        return jnp.concatenate([own, jnp.where(last, fill, after)])

    count = (SAMPLES - extended(missing, 0)).astype(jnp.float32)
    ends = extended(chrom_end, 0)
    seg = jnp.cumsum(ends) - ends
    key = (extended(positions, 0) + 4 * seg).astype(jnp.float32)
    key = jnp.where(last & (jnp.arange(nvar + RIM) >= nvar), FAR, key)
    scale = 1.0 / jnp.sqrt(count)

    def window(table):
        grid = table.reshape(-1, BLK)
        return jnp.stack([grid[k : k + nblk] for k in range(BAND + 1)], axis=1)

    pattern = lax.dynamic_slice_in_dim(pair_pattern, slab * nblk, nblk, 0)
    key_row = jnp.where(pattern[:, :, None] == 1, window(key), FAR).reshape(nblk, 1, WIDTH)
    scale_row = window(scale).reshape(nblk, 1, WIDTH)
    key_own = key[:nvar].reshape(nblk, 1, BLK)
    scale_own = scale[:nvar].reshape(nblk, 1, BLK)

    whole = pl.BlockSpec(memory_space=pltpu.VMEM)
    return pl.pallas_call(
        band_kernel,
        in_specs=[whole] * 6,
        out_specs=anywhere,
        out_shape=jax.ShapeDtypeStruct((nvar, WIDTH), jnp.bfloat16),
        scratch_shapes=[
            pltpu.VMEM((nblk + BAND, SAMPLES, BLK), jnp.bfloat16),
            pltpu.VMEM((nvar, WIDTH), jnp.bfloat16),
            pltpu.SemaphoreType.DMA((nblk,)),
        ],
        compiler_params=pltpu.CompilerParams(vmem_limit_bytes=40 << 20),
    )(mine, count.reshape(-1, 1, BLK), key_row, scale_row, key_own, scale_own)


def solution(mesh):
    placed = (P(AXES, None), P(), P(), P(), P())
    return jax.shard_map(
        on_device,
        mesh=mesh,
        in_specs=placed,
        out_specs=P(AXES, None),
        check_vma=False,
    )
```

time: 69.1 us -> 62.1 us (0.90)
  other arithmetic: 7.51 us -> 2.79 us
  local copies, waits for them, and re-layouts: 4.96 us -> 2.85 us
    concatenate x1 -> x0, other arithmetic: 4.67 us -> none  [on_device(): jnp.concatenate([blocks, rim], axis=2)]
    slice x2 -> x1, local copies, waits for them, and re-layouts: 1.65 us -> 0.08 us  [the longest x1 1.58 us: on_device(): blocks[1:, :, :RIM]]
    pallas_call x1 -> x2, Pallas kernels: 8.44 us -> 8.49 us  [the longest x1 5.66 us: on_device(): pl.pallas_call(band_kernel, in_specs=[whole] * 6, out_specs=anywhere, out...]
  transfers between devices with their start and end apart: 1 -> 1, of which waited for: 1 -> 1; matrix products, arithmetic and copies ran while one was open for 8% -> 9% of each run, Pallas kernels for 0% -> 0%
where the time goes in v1:
time: 62.1 us; the launch traced here: 61.7 us
  waiting for transfers between devices  36 us (58%)
  starting transfers between devices  11.5 us (19%)
  Pallas kernels  8.49 us (14%)
  local copies, waits for them, and re-layouts  2.85 us (5%)
  other arithmetic  2.79 us (4%)
    all_to_all x1, waiting for transfers between devices, on_device(): mine = lax.all_to_all(sent, AXES, split_axis=0, concat_axis=0, tiled=True)  36 us
    all_to_all x1, starting transfers between devices, on_device(): mine = lax.all_to_all(sent, AXES, split_axis=0, concat_axis=0, tiled=True)  11.5 us
    pallas_call x1, Pallas kernels, on_device(): pl.pallas_call(band_kernel, in_specs=[whole] * 6, out_specs=anywhere, out...  5.66 us
    pallas_call x1, Pallas kernels, on_device(): pl.pallas_call(pack_kernel, in_specs=[anywhere], out_specs=anywhere, out_...  2.83 us
    dynamic_slice x3, local copies, waits for them, and re-layouts, extended(): own = lax.dynamic_slice_in_dim(table, row_first, nvar, 0)  2.09 us
    select_n x2, other arithmetic, extended(): return jnp.concatenate([own, jnp.where(last, fill, after)])  1.57 us
  transfers between devices with their start and end apart: 1, of which 1 were waited for; matrix products, arithmetic and copies ran while one was open for 9% of the time, Pallas kernels for 0%

profile of v1, /device:TPU:1, one launch (start us, length us, event | category | flops | bytes accessed | tf_op | source)
XLA Modules:
  0.0 61.7 jit_solution(8516249365245621633)
XLA Ops:
  0.0 2.8 %shard_map.55 = bf16[128,4,3072]{2,1,0:T(4,128)(2,1)} custom-call(bf16[128,4,2048]{2,1,0:T(4,128)(2,1)} %bitcast.12), custom_call_target="tpu_custom_call" | custom-call | tf_op jit(solution)/shard_map/pallas_call | solution.py:130
  2.8 11.5 %all-to-all-start = ((bf16[128,4,3072]{2,1,0:T(4,128)(2,1)}), bf16[128,4,3072]{2,1,0:T(4,128)(2,1)S(1)}, u32[]{:S(2)}, u32[]{:S(2)}) async-start(bf16[128,4,3072]{2,1,0:T(4,128)(2,1)} %shard_map.55), calls=%async_computation | async-start | bytes 6291456 | tf_op jit(solution)/shard_map/all_to_all | solution.py:138
  14.4 0.8 %dynamic-slice_compare_fusion = pred[8,5]{0,1:T(8,128)(4,1)S(1)} fusion(s32[1024,5]{0,1:T(8,128)} %param.9, s32[]{:T(128)S(6)} %select_n.63), kind=kLoop, calls=%fused_computation.9 | loop fusion | flops 40 | bytes 204 | tf_op jit(solution)/shard_map/eq | solution.py:158
  15.1 0.1 copy.9
  15.2 0.7 %dynamic_slice.21 = s32[2048]{0:T(1024)S(1)} dynamic-slice(s32[262144]{0:T(1024)} %param.6, s32[]{:T(128)S(6)} %select_n.59), dynamic_slice_sizes={2048} | dynamic-slice | bytes 16388 | tf_op jit(solution)/shard_map/dynamic_slice | solution.py:141
  15.9 0.7 %dynamic_slice.24 = s32[2048]{0:T(1024)S(1)} dynamic-slice(s32[262144]{0:T(1024)} %param.7, s32[]{:T(128)S(6)} %select_n.59), dynamic_slice_sizes={2048} | dynamic-slice | bytes 16388 | tf_op jit(solution)/shard_map/dynamic_slice | solution.py:141
  16.6 0.7 %dynamic_slice.26 = s32[2048]{0:T(1024)S(1)} dynamic-slice(s32[262144]{0:T(1024)} %param.8, s32[]{:T(128)S(6)} %select_n.59), dynamic_slice_sizes={2048} | dynamic-slice | bytes 16388 | tf_op jit(solution)/shard_map/dynamic_slice | solution.py:141
  17.3 0.8 %dynamic-slice_select_fusion.2 = s32[1024]{0:T(1024)S(1)} fusion(s32[262144]{0:T(1024)} %param.6, s32[]{:T(128)S(6)} %select_n.61, pred[]{:T(512)S(6)} %eq.10), kind=kLoop, calls=%fused_computation.10 | loop fusion | flops 1024 | bytes 8197 | tf_op jit(solution)/shard_map/jit(_where)/select_n | solution.py:144
  18.1 0.8 %dynamic-slice_select_fusion = (s32[1024]{0:T(1024)S(1)}, s32[1024]{0:T(1024)S(1)}) fusion(s32[262144]{0:T(1024)} %param.8, s32[]{:T(128)S(6)} %select_n.61, pred[]{:T(512)S(6)} %eq.10, s32[262144]{0:T(1024)} %param.7), kind=kLoop, calls=%fused_computation.7 | loop fusion | flops 2048 | bytes 16389 | tf_op jit(solution)/shard_map/jit(_where)/select_n | solution.py:144
  18.9 0.3 reduce-window.9
  19.2 0.1 slice.73
  19.3 0.1 slice_reduce_fusion
  19.4 0.1 reshape.238
  19.6 0.1 stack.5
  19.7 0.1 broadcast.145
  19.9 0.1 stack.4
  19.9 0.1 broadcast_select_fusion
  20.1 36.0 %all-to-all-done.dosage_ref = bf16[128,4,3072]{2,1,0:T(4,128)(2,1)S(1)} async-done(((bf16[128,4,3072]{2,1,0:T(4,128)(2,1)}), bf16[128,4,3072]{2,1,0:T(4,128)(2,1)S(1)}, u32[]{:S(2)}, u32[]{:S(2)}) %all-to-all-start) | async-done | bytes 3145760 | tf_op jit(solution)/shard_map/all_to_all | solution.py:138
  56.0 5.7 %shard_map.56 = bf16[2048,1280]{1,0:T(8,128)(2,1)} custom-call(bf16[128,4,3072]{2,1,0:T(4,128)(2,1)S(1)} %all-to-all-done.dosage_ref, f32[12,1,256]{2,1,0:T(1,128)S(1)} %bitcast.11, f32[8,1,1280]{2,1,0:T(1,128)S(1)} %select_n.69.key_row_ref, f32[8,1,1280]{2,1,0:T(1,128)S(1)} %reshape.241.scale_row_ref, f32[8,1,256]{2,1,0:T(1,128)S(1)} %get-tuple-element.14.key_own_ref, ...), custom_call_target="tpu_custom_call" | custom-call | tf_op jit(solution)/shard_map/pallas_call | solution.py:164
  (10 shorter events, 0.3 us)
Async XLA Ops:
  2.8 53.2 %all-to-all-start = ((bf16[128,4,3072]{2,1,0:T(4,128)(2,1)}), bf16[128,4,3072]{2,1,0:T(4,128)(2,1)S(1)}, u32[]{:S(2)}, u32[]{:S(2)}) async-start(bf16[128,4,3072]{2,1,0:T(4,128)(2,1)} %shard_map.55), calls=%async_computation | async-start | bytes 6291456 | tf_op jit(solution)/shard_map/all_to_all | solution.py:138
